TPU v7x, 512 devices: a whole 4x4x16 slice. The times are simulated.
512 devices in a mesh: seq: 128 (over z, y, core), mp: 4 (over x).
Axes of the slice: x: 4, y: 4, z: 16, core: 2. Of those that a mesh axis runs over, the one named last changes fastest.
Arguments:
- queries: bfloat16 [8, 16384], P(None, ('mp', 'seq')), may hold values from -200 to 200
- new_keys: bfloat16 [8, 1024], P(None, 'mp'), may hold values from -4 to 4
- new_values: bfloat16 [8, 1024], P(None, 'mp'), may hold values from -6 to 6
- keys: bfloat16 [512, 512, 1024], P('seq', None, 'mp'), may hold values from -5 to 5
- values: bfloat16 [512, 512, 1024], P('seq', None, 'mp'), may hold values from -6 to 6
- page_table: int32 [8, 64], replicated, may hold values from 0 to 511, as said below
- lengths: int32 [8], replicated, may hold values from 7682 to 32768, as said below
- out_weight: bfloat16 [16384, 16384], P('mp', 'seq'), may hold values from -0.046875 to 0.046875
Outputs:
- mixed: bfloat16 [8, 16384], P(None, 'seq')
Inputs may be any that keep to these rules, and one draw needn't show every extreme that they name: `page_table`: each of the 512 slot numbers appears exactly once in the table. Slot n is local slot n % 4 of the device with index n // 4 along seq. Row r keeps its tokens in the slots of its first ceil(lengths[r] / 512) entries, in order; the slots of its other entries hold no live token. `lengths`: some row has exactly 32768 cached tokens.
All inputs are finite; a program needn't handle non-finite values.
Results may differ from a plain program's by a relative error of at most 0.0051.
Values may be sent and summed in bfloat16 or wider, within the bound.
A program may use at most 64 MiB of HBM per device.

v0:
```python
import math

import jax
import jax.numpy as jnp
from jax import lax
from jax.sharding import PartitionSpec as P

HD = 128


NEG = -1e30


def merge_states(earlier, later):
    highest = jnp.maximum(earlier[0], later[0])
    early_scale = jnp.exp(earlier[0] - highest)
    late_scale = jnp.exp(later[0] - highest)
    return (
        highest,
        earlier[1] * early_scale + later[1] * late_scale,
        earlier[2] * early_scale[..., None] + later[2] * late_scale[..., None],
    )


def shards(queries, new_keys, new_values, keys, values, page_table, lengths, out_weight):
    local_queries = lax.all_gather(queries, "seq", axis=1, tiled=True)
    row_count = local_queries.shape[0]
    slot_count, page_length, kv_width = keys.shape
    local_kv = kv_width // HD
    local_heads = local_queries.shape[1] // HD
    group_size = local_heads // local_kv
    slot_ids = lax.axis_index("seq") * slot_count + jnp.arange(slot_count, dtype=jnp.int32)
    matches = page_table[None, :, :] == slot_ids[:, None, None]
    row_iota = jnp.arange(row_count, dtype=jnp.int32)[None, :, None]
    page_iota = jnp.arange(page_table.shape[1], dtype=jnp.int32)[None, None, :]
    row_of = jnp.sum(jnp.where(matches, row_iota, 0), axis=(1, 2))
    page_of = jnp.sum(jnp.where(matches, page_iota, 0), axis=(1, 2))
    length_of = jnp.take(lengths, row_of)
    positions = page_of[:, None] * page_length + jnp.arange(page_length, dtype=jnp.int32)[None, :]
    live_mask = positions < length_of[:, None]
    row_onehot = jnp.any(matches, axis=2)
    query_heads = jnp.take(local_queries, row_of, axis=0).reshape(
        slot_count, local_kv, group_size, HD
    )
    key_pages = keys.reshape(slot_count, page_length, local_kv, HD)
    value_pages = values.reshape(slot_count, page_length, local_kv, HD)
    scores = jnp.einsum(
        "skgd,stkd->skgt", query_heads, key_pages, preferred_element_type=jnp.float32
    ) / math.sqrt(HD)
    masked = jnp.where(live_mask[:, None, None, :], scores, NEG)
    slot_max = jnp.max(masked, axis=3)
    weights = jnp.where(live_mask[:, None, None, :], jnp.exp(masked - slot_max[..., None]), 0.0)
    slot_total = jnp.sum(weights, axis=3)
    slot_out = jnp.einsum(
        "skgt,stkd->skgd",
        weights.astype(jnp.bfloat16),
        value_pages,
        preferred_element_type=jnp.float32,
    )
    chosen = row_onehot[:, :, None, None]
    row_max = jnp.max(jnp.where(chosen, slot_max[:, None], NEG), axis=0)
    slot_scale = jnp.exp(slot_max - jnp.take(row_max, row_of, axis=0))
    row_total = jnp.sum(jnp.where(chosen, (slot_total * slot_scale)[:, None], 0.0), axis=0)
    row_out = jnp.sum(
        jnp.where(chosen[..., None], (slot_out * slot_scale[..., None])[:, None], 0.0), axis=0
    )
    query_rows = local_queries.reshape(row_count, local_kv, group_size, HD)
    new_key_rows = new_keys.reshape(row_count, local_kv, HD)
    new_scores = jnp.einsum(
        "rkgd,rkd->rkg", query_rows, new_key_rows, preferred_element_type=jnp.float32
    ) / math.sqrt(HD)
    fresh_values = jnp.broadcast_to(
        new_values.reshape(row_count, local_kv, 1, HD).astype(jnp.float32), row_out.shape
    )
    global_max = lax.pmax(row_max, "seq")
    factor = jnp.exp(row_max - global_max)
    row_total, row_out = lax.psum((row_total * factor, row_out * factor[..., None]), "seq")
    row_max = global_max
    fresh = (new_scores, jnp.ones_like(new_scores), fresh_values)
    merged = merge_states((row_max, row_total, row_out), fresh)
    attended = (
        (merged[2] / merged[1][..., None]).reshape(row_count, local_heads * HD).astype(jnp.bfloat16)
    )
    partial_sum = jnp.dot(attended, out_weight, preferred_element_type=jnp.float32)
    return lax.psum(partial_sum, "mp").astype(jnp.bfloat16)


def solution(mesh):
    placed = (
        P(None, ("mp", "seq")),
        P(None, "mp"),
        P(None, "mp"),
        P("seq", None, "mp"),
        P("seq", None, "mp"),
        P(),
        P(),
        P("mp", "seq"),
    )
    return jax.shard_map(
        shards, mesh=mesh, in_specs=placed, out_specs=P(None, "seq"), check_vma=False
    )
```

profile of v0, /device:TPU:1, one launch (start us, length us, event | category | flops | bytes accessed | tf_op | source)
XLA Modules:
  0.0 704.6 jit_solution(994888570316699742)
XLA Ops:
  6.5 0.8 copy-done.3
  7.3 0.3 fusion.18
  7.6 0.2 compare_reduce_fusion
  7.8 0.5 copy-done.5
  8.3 108.4 %all-gather = bf16[128,32,8]{1,2,0:T(8,128)(2,1)S(1)} all-gather(bf16[1,32,8]{1,2,0:T(8,128)(2,1)S(1)} %bitcast.56), channel_id=1, replica_groups=mesh['seq'=128,'mp'=4] {'seq'}, dimensions={0}, use_global_device_ids=true | all-gather | bytes 66048 | tf_op jit(solution)/shard_map/all_gather | solution.py:26
  116.8 0.3 reshape.150
  117.1 0.6 gather_fusion.1
  117.7 0.0 copy-start.1
  117.7 0.6 copy-done.1
  118.3 0.6 gather_fusion
  119.0 0.1 add_compare_fusion
  119.1 0.5 fusion.31
  119.6 0.1 select_reduce_fusion.2
  119.7 250.4 %pmax.7 = f32[8,2,16]{2,0,1:T(8,128)S(1)} all-reduce(f32[8,2,16]{2,0,1:T(8,128)S(1)} %select_reduce_fusion.2), channel_id=1, replica_groups=mesh['seq'=128,'mp'=4] {'seq'}, use_global_device_ids=true, to_apply=%region_6.7 | all-reduce | flops 256 | bytes 2048 | tf_op jit(solution)/shard_map/pmax | solution.py:75
  370.1 0.2 fusion.5
  370.3 0.6 gather_fusion.2
  370.8 0.1 fusion.30
  370.9 0.0 copy-start.2
  371.0 0.3 convolution_multiply_fusion.1
  371.3 0.1 select_reduce_fusion
  371.4 0.1 select_reduce_fusion.1
  371.5 0.8 broadcast_multiply_fusion
  372.3 0.0 all-reduce.2.cloned.1.call-update
  372.3 0.0 copy-start.7
  372.3 253.6 %psum.22 = f32[8,2,16]{2,0,1:T(8,128)S(1)} all-reduce(f32[8,2,16]{2,0,1:T(8,128)S(1)} %get-tuple-element.10), channel_id=1, replica_groups=mesh['seq'=128,'mp'=4] {'seq'}, use_global_device_ids=true, to_apply=%region_10.11 | all-reduce | flops 256 | bytes 2048 | tf_op jit(solution)/shard_map/psum | solution.py:77
  625.9 0.1 fusion.14
  626.1 0.0 copy-start.4
  626.1 0.7 copy-done.4
  626.8 60.6 %all-reduce.2.cloned.1.call-done = f32[8,2,16,128]{3,2,1,0:T(8,128)} async-done(((f32[8,2,16,128]{3,2,1,0:T(8,128)}), f32[8,2,16,128]{3,2,1,0:T(8,128)}) %all-reduce.2.cloned.1.call-update) | async-done | bytes 131088 | tf_op jit(solution)/shard_map/psum | solution.py:77
  687.4 1.1 divide_convert_fusion
  688.5 0.2 fusion.11
  688.7 9.1 %psum.23 = bf16[8,128]{1,0:T(8,128)(2,1)} all-reduce(f32[8,128]{1,0:T(8,128)S(1)} %fusion.11), channel_id=1, replica_groups=mesh['seq'=128,'mp'=4] {'mp'}, use_global_device_ids=true, to_apply=%region_11.12 | all-reduce | flops 1024 | bytes 6144 | tf_op jit(solution)/shard_map/psum | solution.py:85
  (24 shorter events, 0.2 us)
Async XLA Ops:
  6.5 112.5 %copy-start = (bf16[4,512,256]{2,1,0:T(8,128)(2,1)S(1)}, bf16[4,512,256]{2,1,0:T(8,128)(2,1)}, u32[]{:S(2)}) copy-start(bf16[4,512,256]{2,1,0:T(8,128)(2,1)} %param.11) | copy-start | bytes 3145732
  6.5 680.9 %all-reduce.2.cloned.1.call-start = ((), (), s32[]{:S(2)}) async-start(), calls=%async_computation | async-start | bytes 262144 | tf_op jit(solution)/shard_map/psum | solution.py:77
  6.5 0.8 copy-start.3
  7.6 0.7 copy-start.5
  117.7 0.7 copy-start.1
  118.3 252.6 %copy-start.6 = (bf16[4,512,256]{2,1,0:T(8,128)(2,1)S(1)}, bf16[4,512,256]{2,1,0:T(8,128)(2,1)}, u32[]{:S(2)}) copy-start(bf16[4,512,256]{2,1,0:T(8,128)(2,1)} %param.12) | copy-start | bytes 3145732
  370.9 317.5 %copy-start.2 = (bf16[4096,128]{1,0:T(8,128)(2,1)S(1)}, bf16[4096,128]{1,0:T(8,128)(2,1)}, u32[]{:S(2)}) copy-start(bf16[4096,128]{1,0:T(8,128)(2,1)} %param.15) | copy-start | bytes 3145732
  372.3 253.7 %copy-start.7 = (bf16[8,256]{1,0:T(8,128)(2,1)S(1)}, bf16[8,256]{1,0:T(8,128)(2,1)}, u32[]{:S(2)}) copy-start(bf16[8,256]{1,0:T(8,128)(2,1)} %param.9) | copy-start | bytes 12292
  626.1 0.7 copy-start.4
Sparse Core Ops, SparseCore 0:
  372.4 314.9 all-reduce.1
where the time goes:
time: 707 us; the launch traced here: 705 us
  blocking collectives  622 us (88%)
  waiting for transfers between devices  60.6 us (9%)
  between operations  13.6 us (2%)
    psum x1, blocking collectives, shards(): lax.psum((row_total * factor, row_out * factor[..., None]), 'seq')  254 us
    pmax x1, blocking collectives, shards(): global_max = lax.pmax(row_max, 'seq')  250 us
    all_gather x1, blocking collectives, shards(): local_queries = lax.all_gather(queries, 'seq', axis=1, tiled=True)  108 us
    psum x1, waiting for transfers between devices, shards(): lax.psum((row_total * factor, row_out * factor[..., None]), 'seq')  60.6 us
  transfers between devices with their start and end apart: 1, of which 1 were waited for; matrix products, arithmetic and copies ran while one was open for 0% of the time, Pallas kernels for 0%

commit v1 on v0

v1 whole, which is shorter than its diff:
```python
import math

import jax
import jax.numpy as jnp
from jax import lax
from jax.experimental import pallas as pl
from jax.experimental.pallas import tpu as pltpu
from jax.sharding import PartitionSpec as P

MESH = pl.DeviceIdType.MESH
NEG = -1e30
HD = 128
ROWS = 8
PLANES = 16
LOCAL = 8
XS = 4
SLOTS = 4
PAGE = 512
F32 = jnp.float32
BF16 = jnp.bfloat16


def iota(shape, axis):
    return lax.broadcasted_iota(jnp.int32, shape, axis)


def kernel(
    q_ref, nk_ref, nv_ref, pt_ref, len_ref, k_hbm, v_hbm, w_hbm, out_ref,
    k_buf, v_buf, w_buf, zq, qbuf, sbuf, rbuf, zo, zs, abuf, xbuf,
    load_sem, send_sem, recv_sem,
):
    i = lax.axis_index("seq")
    x = lax.axis_index("mp")
    z = i // LOCAL
    p = lax.rem(i, LOCAL)

    z_steps = sorted(range(1, PLANES), key=lambda k: -min(k, PLANES - k))
    p_steps = (4, 5, 2, 3, 6, 7, 1)
    x_steps = (2, 1, 3)

    def z_peer(k):
        return {"seq": lax.rem(z + k, PLANES) * LOCAL + p}

    def p_index(k):
        return lax.rem(p + k, LOCAL)

    def p_peer(k):
        return {"seq": z * LOCAL + p_index(k)}

    def x_peer(k):
        return {"mp": lax.rem(x + k, XS)}

    peers = [z_peer(k) for k in z_steps]
    peers += [p_peer(k) for k in p_steps]
    peers += [x_peer(k) for k in x_steps]
    barrier = pltpu.get_barrier_semaphore()
    for peer in peers:
        pl.semaphore_signal(barrier, inc=1, device_id=peer, device_id_type=MESH)

    loads = [
        pltpu.make_async_copy(src, dst, load_sem.at[n])
        for n, (src, dst) in enumerate(((k_hbm, k_buf), (v_hbm, v_buf), (w_hbm, w_buf)))
    ]
    for load in loads:
        load.start()

    def send(src, dst, n, peer):
        pltpu.make_async_remote_copy(
            src_ref=src, dst_ref=dst, send_sem=send_sem.at[n], recv_sem=recv_sem.at[n],
            device_id=peer, device_id_type=MESH,
        ).start()

    def wait(ref, sems, n):
        pltpu.make_async_copy(ref, ref, sems.at[n]).wait()

    spread = (iota((32, 128), 0) == (iota((32, 128), 1) & 31)).astype(BF16)
    wide = jnp.dot(q_ref[...], spread, preferred_element_type=F32)
    row8 = iota((8, 128), 0)
    mine = jnp.where((iota((8, 128), 1) >> 5) == (row8 & 3), wide, 0.0)
    low = jnp.sum(jnp.where(row8 < 4, mine, 0.0), axis=0, keepdims=True)
    high = jnp.sum(jnp.where(row8 < 4, 0.0, mine), axis=0, keepdims=True)
    zq[z] = jnp.where(row8 == 0, low, jnp.where(row8 == 1, high, 0.0))

    pl.semaphore_wait(barrier, len(peers))
    for k in z_steps:
        send(zq.at[z], zq.at[z], 0, z_peer(k))

    lane64 = iota((128, 64), 1)
    rho = iota((128, 64), 0)
    my_slot = i * SLOTS + ((rho >> 2) & 3)
    plane_slot = z * (LOCAL * SLOTS) + (rho >> 2)
    row_acc = jnp.zeros((128, 64), F32)
    live_acc = jnp.zeros((128, 64), F32)
    plane_acc = jnp.zeros((128, 64), F32)
    for r in range(ROWS):
        entry = pt_ref[r : r + 1, :]
        hit = entry == my_slot
        row_acc += jnp.where(hit, float(r), 0.0)
        live_acc += jnp.where(hit, (len_ref[r] - lane64 * PAGE).astype(F32), 0.0)
        plane_acc += jnp.where(entry == plane_slot, float(r), 0.0)
    row_of = jnp.sum(row_acc, axis=1, keepdims=True).astype(jnp.int32)
    live_of = jnp.sum(live_acc, axis=1, keepdims=True).astype(jnp.int32)
    plane_row = jnp.sum(plane_acc, axis=1, keepdims=True).astype(jnp.int32)

    rho1 = iota((128, 1), 0)
    tau1 = iota((32, 1), 0)
    head = jnp.concatenate([4 * (rho1 >> 4) + (rho1 & 3), 4 * p + (tau1 >> 3)], axis=0)
    row = jnp.concatenate([row_of, tau1 & 7], axis=0)
    start = (head & 1) * 128 + (row >> 2) * 16 + (head >> 1)
    column = iota((160, 256), 1)
    select = jnp.concatenate(
        [(column == start + quarter * 32).astype(F32) for quarter in range(4)], axis=0
    ).astype(BF16)
    lane160 = iota((160, 128), 1)
    in_row = (lane160 >> 5) == (row & 3)
    l0, l1 = iota((128, 128), 0), iota((128, 128), 1)
    same = (l0 & 31) == (l1 & 31)
    fold = [(same & ((l1 >> 5) == quarter)).astype(F32).astype(BF16) for quarter in range(4)]
    slot_of = (rho1 >> 2) & 3
    match = ((l0 & 3) == ((l1 >> 3) & 3)) & (plane_row == (l1 & 7))
    first_kv = p < 4
    nk = jnp.where(first_kv, nk_ref[:, :HD].astype(F32), nk_ref[:, HD:].astype(F32))
    nv = jnp.where(first_kv, nv_ref[:, :HD].astype(F32), nv_ref[:, HD:].astype(F32))
    nk = jnp.concatenate([nk] * 4, axis=0)
    nv = jnp.concatenate([nv] * 4, axis=0)

    wait(zq.at[pl.ds(0, PLANES - 1)], recv_sem, 0)
    qbuf[p] = jnp.concatenate([zq[:, 0, :], zq[:, 1, :]], axis=0)
    for k in p_steps:
        send(qbuf.at[p], qbuf.at[p], 1, p_peer(k))
    wait(qbuf.at[pl.ds(0, LOCAL - 1)], recv_sem, 1)

    gathered = qbuf[...].reshape(256, 128).astype(BF16)
    picked = jnp.dot(select, gathered, preferred_element_type=F32)
    queries = jnp.zeros((160, 128), F32)
    for quarter in range(4):
        part = jnp.where(in_row, picked[quarter * 160 : (quarter + 1) * 160], 0.0).astype(BF16)
        queries += jnp.dot(part, fold[quarter], preferred_element_type=F32)
    fresh_queries = queries[128:]
    queries = queries[:128]

    loads[0].wait()
    scores = jnp.zeros((128, PAGE), F32)
    first_half = rho1 < 64
    for s in range(SLOTS):
        here = slot_of == s
        block = jnp.concatenate(
            [
                jnp.where(here & first_half, queries, 0.0),
                jnp.where(here & jnp.logical_not(first_half), queries, 0.0),
            ],
            axis=1,
        ).astype(BF16)
        scores += lax.dot_general(
            block, k_buf[s], (((1,), (1,)), ((), ())), preferred_element_type=F32
        )
    scale = 1.0 / math.sqrt(HD)
    live = iota((128, PAGE), 1) < live_of
    masked = jnp.where(live, scores * scale, NEG)
    page_max = jnp.max(masked, axis=1, keepdims=True)
    weights = jnp.where(live, jnp.exp(masked - page_max), 0.0)
    page_total = jnp.sum(weights, axis=1, keepdims=True)
    loads[1].wait()
    outs = jnp.zeros((128, 2 * HD), F32)
    for s in range(SLOTS):
        outs += jnp.dot(
            jnp.where(slot_of == s, weights, 0.0).astype(BF16), v_buf[s], preferred_element_type=F32
        )
    stats = jnp.where(l1 < 64, page_max, page_total)
    for n in range(LOCAL):
        half = n // 4
        sbuf[n, 0:16, :] = outs[n * 16 : (n + 1) * 16, half * HD : (half + 1) * HD]
        sbuf[n, 16:32, :] = stats[n * 16 : (n + 1) * 16]
    for k in p_steps:
        send(sbuf.at[p_index(k)], rbuf.at[p], 2, p_peer(k))
    rbuf[p] = sbuf[p]
    fresh_scores = jnp.sum(fresh_queries * nk, axis=1, keepdims=True) * scale
    wait(rbuf.at[pl.ds(0, LOCAL - 1)], recv_sem, 2)

    parts = rbuf[:, 0:16, :].reshape(128, 128)
    stats = rbuf[:, 16:32, :].reshape(128, 128)
    turned = pltpu.roll(stats, 64, 1)
    part_max = jnp.where(l1 < 64, stats, turned)
    part_total = jnp.where(l1 < 64, turned, stats)
    plane_max = jnp.max(jnp.where(match, part_max, NEG), axis=0, keepdims=True)
    factor = jnp.where(match, jnp.exp(part_max - plane_max), 0.0)
    plane_total = jnp.sum(factor * part_total, axis=0, keepdims=True)
    merged = jnp.dot(
        factor.T[:32], parts, preferred_element_type=F32, precision=lax.Precision.HIGHEST
    )
    zo[z] = merged.astype(BF16)
    lane1 = iota((1, 128), 1)
    zs[z] = jnp.where(lane1 < 32, plane_max, plane_total)
    for k in z_steps:
        send(zs.at[z], zs.at[z], 3, z_peer(k))
        send(zo.at[z], zo.at[z], 4, z_peer(k))
    wait(zs.at[pl.ds(0, PLANES - 1)], recv_sem, 3)
    wait(zo.at[pl.ds(0, PLANES - 1)], recv_sem, 4)

    table = jnp.full((128, 128), NEG, F32)
    for n in range(PLANES):
        table = jnp.where(l0 == n, zs[n], table)
    table = table.T
    lane32 = iota((32, 128), 1)
    maxima = jnp.where(lane32 < PLANES, table[:32], NEG)
    totals = jnp.where(lane32 < PLANES, table[32:64], 0.0)
    top = jnp.maximum(jnp.max(maxima, axis=1, keepdims=True), fresh_scores)
    factor = jnp.exp(maxima - top)
    fresh_factor = jnp.exp(fresh_scores - top)
    total = jnp.sum(factor * totals, axis=1, keepdims=True) + fresh_factor
    mixed = fresh_factor * nv
    for n in range(PLANES):
        mixed += factor[:, n : n + 1] * zo[n].astype(F32)
    abuf[p] = (mixed / total).astype(BF16)
    for k in p_steps:
        send(abuf.at[p], abuf.at[p], 5, p_peer(k))
    loads[2].wait()
    wait(abuf.at[pl.ds(0, LOCAL - 1)], recv_sem, 5)

    acc = jnp.zeros((ROWS, 128), F32)
    for n in range(LOCAL):
        block = abuf[n].astype(F32)
        flat = jnp.concatenate([block[8 * h : 8 * h + 8] for h in range(4)], axis=1).astype(BF16)
        acc += jnp.dot(flat, w_buf[n * 512 : (n + 1) * 512, :], preferred_element_type=F32)
    xbuf[x] = acc
    for k in x_steps:
        send(xbuf.at[x], xbuf.at[x], 6, x_peer(k))
    wait(xbuf.at[pl.ds(0, XS - 1)], recv_sem, 6)
    out_ref[...] = ((xbuf[0] + xbuf[1]) + (xbuf[2] + xbuf[3])).astype(out_ref.dtype)

    wait(zq.at[pl.ds(0, PLANES - 1)], send_sem, 0)
    wait(qbuf.at[pl.ds(0, LOCAL - 1)], send_sem, 1)
    wait(rbuf.at[pl.ds(0, LOCAL - 1)], send_sem, 2)
    wait(zs.at[pl.ds(0, PLANES - 1)], send_sem, 3)
    wait(zo.at[pl.ds(0, PLANES - 1)], send_sem, 4)
    wait(abuf.at[pl.ds(0, LOCAL - 1)], send_sem, 5)
    wait(xbuf.at[pl.ds(0, XS - 1)], send_sem, 6)


def shards(queries, new_keys, new_values, keys, values, page_table, lengths, out_weight):
    vmem = pl.BlockSpec(memory_space=pltpu.VMEM)
    smem = pl.BlockSpec(memory_space=pltpu.SMEM)
    hbm = pl.BlockSpec(memory_space=pl.ANY)
    return pl.pallas_call(
        kernel,
        out_shape=jax.ShapeDtypeStruct((ROWS, out_weight.shape[1]), BF16),
        in_specs=[vmem, vmem, vmem, vmem, smem, hbm, hbm, hbm],
        out_specs=vmem,
        scratch_shapes=[
            pltpu.VMEM(keys.shape, BF16),
            pltpu.VMEM(values.shape, BF16),
            pltpu.VMEM(out_weight.shape, BF16),
            pltpu.VMEM((PLANES, 8, 128), F32),
            pltpu.VMEM((LOCAL, 32, 128), F32),
            pltpu.VMEM((LOCAL, 32, 128), F32),
            pltpu.VMEM((LOCAL, 32, 128), F32),
            pltpu.VMEM((PLANES, 32, 128), BF16),
            pltpu.VMEM((PLANES, 1, 128), F32),
            pltpu.VMEM((LOCAL, 32, 128), BF16),
            pltpu.VMEM((XS, ROWS, 128), F32),
            pltpu.SemaphoreType.DMA((3,)),
            pltpu.SemaphoreType.DMA((7,)),
            pltpu.SemaphoreType.DMA((7,)),
        ],
        compiler_params=pltpu.CompilerParams(
            collective_id=0, has_side_effects=True, vmem_limit_bytes=48 * 1024 * 1024
        ),
    )(queries, new_keys, new_values, page_table, lengths, keys, values, out_weight)


def solution(mesh):
    placed = (
        P(None, ("mp", "seq")),
        P(None, "mp"),
        P(None, "mp"),
        P("seq", None, "mp"),
        P("seq", None, "mp"),
        P(),
        P(),
        P("mp", "seq"),
    )
    return jax.shard_map(
        shards, mesh=mesh, in_specs=placed, out_specs=P(None, "seq"), check_vma=False
    )
```

time: 707 us -> 59.5 us (0.08)
  blocking collectives: 622 us -> 0 us
  waiting for transfers between devices: 60.6 us -> 0 us
  Pallas kernels: 0 us -> 51.5 us
  between operations: 13.6 us -> 0.02 us
    psum x2 -> x0, blocking collectives: 263 us -> none  [the longest x1 254 us: shards(): lax.psum((row_total * factor, row_out * factor[..., None]), 'seq')]
    pmax x1 -> x0, blocking collectives: 250 us -> none  [shards(): global_max = lax.pmax(row_max, 'seq')]
    all_gather x1 -> x0, blocking collectives: 108 us -> none  [shards(): local_queries = lax.all_gather(queries, 'seq', axis=1, tiled=True)]
    psum x1 -> x0, waiting for transfers between devices: 60.6 us -> none  [shards(): lax.psum((row_total * factor, row_out * factor[..., None]), 'seq')]
    pallas_call x0 -> x1, Pallas kernels: none -> 51.5 us  [shards(): pl.pallas_call(kernel, out_shape=jax.ShapeDtypeStruct((ROWS, out_weight.s...]
  transfers between devices with their start and end apart: 1 -> 0, of which waited for: 1 -> 0; matrix products, arithmetic and copies ran while one was open for 0% -> 0% of each run, Pallas kernels for 0% -> 0%
where the time goes in v1:
time: 59.5 us; the launch traced here: 59.1 us
  Pallas kernels  51.5 us (87%)
  local copies, waits for them, and re-layouts  7.65 us (13%)
    pallas_call x1, Pallas kernels, shards(): pl.pallas_call(kernel, out_shape=jax.ShapeDtypeStruct((ROWS, out_weight.s...  51.5 us
    unnamed x17, local copies, waits for them, and re-layouts  7.65 us

profile of v1, /device:TPU:1, one launch (start us, length us, event | category | flops | bytes accessed | tf_op | source)
XLA Modules:
  0.0 59.1 jit_solution(16494380663029440519)
XLA Ops:
  0.0 0.0 copy-start
  0.0 1.2 %copy-done = bf16[4,512,256]{2,1,0:T(8,128)(2,1)S(1)} copy-done((bf16[4,512,256]{2,1,0:T(8,128)(2,1)S(1)}, bf16[4,512,256]{2,1,0:T(8,128)(2,1)}, u32[]{:S(2)}) %copy-start) | copy-done | bytes 1048600
  1.2 0.0 copy-start.1
  1.2 1.2 %copy-done.1 = bf16[4,512,256]{2,1,0:T(8,128)(2,1)S(1)} copy-done((bf16[4,512,256]{2,1,0:T(8,128)(2,1)S(1)}, bf16[4,512,256]{2,1,0:T(8,128)(2,1)}, u32[]{:S(2)}) %copy-start.1) | copy-done | bytes 1048600
  2.5 0.0 copy-start.2
  2.5 1.2 %copy-done.2 = bf16[4096,128]{1,0:T(8,128)(2,1)S(1)} copy-done((bf16[4096,128]{1,0:T(8,128)(2,1)S(1)}, bf16[4096,128]{1,0:T(8,128)(2,1)}, u32[]{:S(2)}) %copy-start.2) | copy-done | bytes 1048600
  3.7 0.0 copy-start.3
  3.7 0.7 %copy-done.3 = bf16[8,256]{1,0:T(8,128)(2,1)S(1)} copy-done((bf16[8,256]{1,0:T(8,128)(2,1)S(1)}, bf16[8,256]{1,0:T(8,128)(2,1)}, u32[]{:S(2)}) %copy-start.3) | copy-done | bytes 4120
  4.4 0.0 copy-start.4
  4.4 0.7 %copy-done.4 = bf16[8,256]{1,0:T(8,128)(2,1)S(1)} copy-done((bf16[8,256]{1,0:T(8,128)(2,1)S(1)}, bf16[8,256]{1,0:T(8,128)(2,1)}, u32[]{:S(2)}) %copy-start.4) | copy-done | bytes 4120
  5.1 0.0 copy-start.5
  5.1 0.7 %copy-done.5 = s32[8,64]{1,0:T(8,128)S(1)} copy-done((s32[8,64]{1,0:T(8,128)S(1)}, s32[8,64]{1,0:T(8,128)}, u32[]{:S(2)}) %copy-start.5) | copy-done | bytes 2072
  5.7 0.0 copy-start.6
  5.7 0.7 %copy-done.6 = bf16[8,32]{1,0:T(8,128)(2,1)S(1)} copy-done((bf16[8,32]{1,0:T(8,128)(2,1)S(1)}, bf16[8,32]{1,0:T(8,128)(2,1)}, u32[]{:S(2)}) %copy-start.6) | copy-done | bytes 536
  6.4 0.0 copy-start.7
  6.4 0.7 %copy-done.7 = s32[8]{0:T(128)S(1)} copy-done((s32[8]{0:T(128)S(1)}, s32[8]{0:T(128)}, u32[]{:S(2)}) %copy-start.7) | copy-done | bytes 56
  7.1 51.5 %shard_map.82 = bf16[8,128]{1,0:T(8,128)(2,1)S(1)} custom-call(bf16[8,32]{1,0:T(8,128)(2,1)S(1)} %copy-done.6, bf16[8,256]{1,0:T(8,128)(2,1)S(1)} %copy-done.3, bf16[8,256]{1,0:T(8,128)(2,1)S(1)} %copy-done.4, s32[8,64]{1,0:T(8,128)S(1)} %copy-done.5, s32[8]{0:T(128)S(1)} %copy-done.7, bf16[4,512,256]{2,1,0:T(8,128)(2,1)S(1)} %copy-done, ...), custom_call_target="tpu_custom_call" | custom-call | tf_op jit(solution)/shard_map/pallas_call | solution.py:244
  58.6 0.6 copy.10
Async XLA Ops:
  0.0 1.2 %copy-start = (bf16[4,512,256]{2,1,0:T(8,128)(2,1)S(1)}, bf16[4,512,256]{2,1,0:T(8,128)(2,1)}, u32[]{:S(2)}) copy-start(bf16[4,512,256]{2,1,0:T(8,128)(2,1)} %k_hbm.1) | copy-start | bytes 3145732
  1.2 1.2 %copy-start.1 = (bf16[4,512,256]{2,1,0:T(8,128)(2,1)S(1)}, bf16[4,512,256]{2,1,0:T(8,128)(2,1)}, u32[]{:S(2)}) copy-start(bf16[4,512,256]{2,1,0:T(8,128)(2,1)} %v_hbm.1) | copy-start | bytes 3145732
  2.5 1.2 %copy-start.2 = (bf16[4096,128]{1,0:T(8,128)(2,1)S(1)}, bf16[4096,128]{1,0:T(8,128)(2,1)}, u32[]{:S(2)}) copy-start(bf16[4096,128]{1,0:T(8,128)(2,1)} %w_hbm.1) | copy-start | bytes 3145732
  3.7 0.7 %copy-start.3 = (bf16[8,256]{1,0:T(8,128)(2,1)S(1)}, bf16[8,256]{1,0:T(8,128)(2,1)}, u32[]{:S(2)}) copy-start(bf16[8,256]{1,0:T(8,128)(2,1)} %nk_ref.1) | copy-start | bytes 12292
  4.4 0.7 %copy-start.4 = (bf16[8,256]{1,0:T(8,128)(2,1)S(1)}, bf16[8,256]{1,0:T(8,128)(2,1)}, u32[]{:S(2)}) copy-start(bf16[8,256]{1,0:T(8,128)(2,1)} %nv_ref.1) | copy-start | bytes 12292
  5.1 0.7 %copy-start.5 = (s32[8,64]{1,0:T(8,128)S(1)}, s32[8,64]{1,0:T(8,128)}, u32[]{:S(2)}) copy-start(s32[8,64]{1,0:T(8,128)} %pt_ref.1) | copy-start | bytes 6148
  5.7 0.7 %copy-start.6 = (bf16[8,32]{1,0:T(8,128)(2,1)S(1)}, bf16[8,32]{1,0:T(8,128)(2,1)}, u32[]{:S(2)}) copy-start(bf16[8,32]{1,0:T(8,128)(2,1)} %q_ref.1) | copy-start | bytes 1540
  6.4 0.7 %copy-start.7 = (s32[8]{0:T(128)S(1)}, s32[8]{0:T(128)}, u32[]{:S(2)}) copy-start(s32[8]{0:T(128)} %len_ref.1) | copy-start | bytes 100

commit v2 on v1

--- a/solution.py
+++ b/solution.py
@@ -25,9 +25,9 @@
 
 
 def kernel(
-    q_ref, nk_ref, nv_ref, pt_ref, len_ref, k_hbm, v_hbm, w_hbm, out_ref,
-    k_buf, v_buf, w_buf, zq, qbuf, sbuf, rbuf, zo, zs, abuf, xbuf,
-    load_sem, send_sem, recv_sem,
+    q_hbm, nk_hbm, nv_hbm, pt_hbm, len_hbm, k_hbm, v_hbm, w_hbm, out_ref,
+    q_ref, nk_ref, nv_ref, pt_ref, len_ref, k_buf, v_buf, w_buf, pbuf, zq, sbuf, rbuf, zo, zs, abuf, xbuf,
+    load_sem, send_sem, recv_sem, ready_sem,
 ):
     i = lax.axis_index("seq")
     x = lax.axis_index("mp")
@@ -35,14 +35,14 @@
     p = lax.rem(i, LOCAL)
 
     z_steps = sorted(range(1, PLANES), key=lambda k: -min(k, PLANES - k))
-    p_steps = (4, 5, 2, 3, 6, 7, 1)
+    p_steps = ((2, 0), (2, 1), (1, 0), (3, 0), (1, 1), (3, 1), (0, 1))
     x_steps = (2, 1, 3)
 
     def z_peer(k):
         return {"seq": lax.rem(z + k, PLANES) * LOCAL + p}
 
     def p_index(k):
-        return lax.rem(p + k, LOCAL)
+        return lax.rem((p >> 1) + k[0], 4) * 2 + lax.rem((p & 1) + k[1], 2)
 
     def p_peer(k):
         return {"seq": z * LOCAL + p_index(k)}
@@ -50,7 +50,7 @@
     def x_peer(k):
         return {"mp": lax.rem(x + k, XS)}
 
-    peers = [z_peer(k) for k in z_steps]
+    peers = [z_peer(k) for k in z_steps if min(k, PLANES - k) <= 4]
     peers += [p_peer(k) for k in p_steps]
     peers += [x_peer(k) for k in x_steps]
     barrier = pltpu.get_barrier_semaphore()
@@ -59,32 +59,39 @@
 
     loads = [
         pltpu.make_async_copy(src, dst, load_sem.at[n])
-        for n, (src, dst) in enumerate(((k_hbm, k_buf), (v_hbm, v_buf), (w_hbm, w_buf)))
+        for n, (src, dst) in enumerate(
+            (
+                (q_hbm, q_ref), (pt_hbm, pt_ref), (len_hbm, len_ref), (nk_hbm, nk_ref),
+                (nv_hbm, nv_ref), (k_hbm, k_buf), (v_hbm, v_buf), (w_hbm, w_buf),
+            )
+        )
     ]
     for load in loads:
         load.start()
 
-    def send(src, dst, n, peer):
+    def send(src, dst, n, peer, m=None):
         pltpu.make_async_remote_copy(
-            src_ref=src, dst_ref=dst, send_sem=send_sem.at[n], recv_sem=recv_sem.at[n],
+            src_ref=src, dst_ref=dst, send_sem=send_sem.at[n], recv_sem=recv_sem.at[n if m is None else m],
             device_id=peer, device_id_type=MESH,
         ).start()
 
     def wait(ref, sems, n):
         pltpu.make_async_copy(ref, ref, sems.at[n]).wait()
 
+    loads[0].wait()
+    lane8 = iota((8, 128), 1)
     spread = (iota((32, 128), 0) == (iota((32, 128), 1) & 31)).astype(BF16)
     wide = jnp.dot(q_ref[...], spread, preferred_element_type=F32)
-    row8 = iota((8, 128), 0)
-    mine = jnp.where((iota((8, 128), 1) >> 5) == (row8 & 3), wide, 0.0)
-    low = jnp.sum(jnp.where(row8 < 4, mine, 0.0), axis=0, keepdims=True)
-    high = jnp.sum(jnp.where(row8 < 4, 0.0, mine), axis=0, keepdims=True)
-    zq[z] = jnp.where(row8 == 0, low, jnp.where(row8 == 1, high, 0.0))
+    pbuf[p] = jnp.where((lane8 >> 5) == (p & 3), wide, 0.0)
 
     pl.semaphore_wait(barrier, len(peers))
-    for k in z_steps:
-        send(zq.at[z], zq.at[z], 0, z_peer(k))
-
+    for k in (4, 12):
+        pl.semaphore_signal(ready_sem, inc=1, device_id=z_peer(k), device_id_type=MESH)
+    for k in p_steps:
+        send(pbuf.at[p], pbuf.at[p], 0, p_peer(k))
+
+    for load in loads[1:5]:
+        load.wait()
     lane64 = iota((128, 64), 1)
     rho = iota((128, 64), 0)
     my_slot = i * SLOTS + ((rho >> 2) & 3)
@@ -106,16 +113,9 @@
     tau1 = iota((32, 1), 0)
     head = jnp.concatenate([4 * (rho1 >> 4) + (rho1 & 3), 4 * p + (tau1 >> 3)], axis=0)
     row = jnp.concatenate([row_of, tau1 & 7], axis=0)
-    start = (head & 1) * 128 + (row >> 2) * 16 + (head >> 1)
-    column = iota((160, 256), 1)
-    select = jnp.concatenate(
-        [(column == start + quarter * 32).astype(F32) for quarter in range(4)], axis=0
-    ).astype(BF16)
-    lane160 = iota((160, 128), 1)
-    in_row = (lane160 >> 5) == (row & 3)
+    start = (head >> 1) * 16 + (head & 1) * 8 + row
+    select = (iota((160, 256), 1) == start).astype(F32).astype(BF16)
     l0, l1 = iota((128, 128), 0), iota((128, 128), 1)
-    same = (l0 & 31) == (l1 & 31)
-    fold = [(same & ((l1 >> 5) == quarter)).astype(F32).astype(BF16) for quarter in range(4)]
     slot_of = (rho1 >> 2) & 3
     match = ((l0 & 3) == ((l1 >> 3) & 3)) & (plane_row == (l1 & 7))
     first_kv = p < 4
@@ -124,22 +124,20 @@
     nk = jnp.concatenate([nk] * 4, axis=0)
     nv = jnp.concatenate([nv] * 4, axis=0)
 
-    wait(zq.at[pl.ds(0, PLANES - 1)], recv_sem, 0)
-    qbuf[p] = jnp.concatenate([zq[:, 0, :], zq[:, 1, :]], axis=0)
-    for k in p_steps:
-        send(qbuf.at[p], qbuf.at[p], 1, p_peer(k))
-    wait(qbuf.at[pl.ds(0, LOCAL - 1)], recv_sem, 1)
-
-    gathered = qbuf[...].reshape(256, 128).astype(BF16)
-    picked = jnp.dot(select, gathered, preferred_element_type=F32)
-    queries = jnp.zeros((160, 128), F32)
-    for quarter in range(4):
-        part = jnp.where(in_row, picked[quarter * 160 : (quarter + 1) * 160], 0.0).astype(BF16)
-        queries += jnp.dot(part, fold[quarter], preferred_element_type=F32)
+    wait(pbuf.at[pl.ds(0, LOCAL - 1)], recv_sem, 0)
+    low = (pbuf[0] + pbuf[1]) + (pbuf[2] + pbuf[3])
+    high = (pbuf[4] + pbuf[5]) + (pbuf[6] + pbuf[7])
+    zq[z] = jnp.concatenate([low, high], axis=0).astype(BF16)
+    pl.semaphore_wait(ready_sem, 2)
+    for k in z_steps:
+        send(zq.at[z], zq.at[z], 1, z_peer(k))
+    wait(zq.at[pl.ds(0, PLANES - 1)], recv_sem, 1)
+
+    queries = jnp.dot(select, zq[...].reshape(256, 128), preferred_element_type=F32)
     fresh_queries = queries[128:]
     queries = queries[:128]
 
-    loads[0].wait()
+    loads[5].wait()
     scores = jnp.zeros((128, PAGE), F32)
     first_half = rho1 < 64
     for s in range(SLOTS):
@@ -160,7 +158,7 @@
     page_max = jnp.max(masked, axis=1, keepdims=True)
     weights = jnp.where(live, jnp.exp(masked - page_max), 0.0)
     page_total = jnp.sum(weights, axis=1, keepdims=True)
-    loads[1].wait()
+    loads[6].wait()
     outs = jnp.zeros((128, 2 * HD), F32)
     for s in range(SLOTS):
         outs += jnp.dot(
@@ -212,24 +210,29 @@
     for n in range(PLANES):
         mixed += factor[:, n : n + 1] * zo[n].astype(F32)
     abuf[p] = (mixed / total).astype(BF16)
-    for k in p_steps:
-        send(abuf.at[p], abuf.at[p], 5, p_peer(k))
-    loads[2].wait()
-    wait(abuf.at[pl.ds(0, LOCAL - 1)], recv_sem, 5)
-
-    acc = jnp.zeros((ROWS, 128), F32)
-    for n in range(LOCAL):
+    for n, k in enumerate(p_steps):
+        send(abuf.at[p], abuf.at[p], 5, p_peer(k), 7 + n)
+
+    def project(n):
         block = abuf[n].astype(F32)
         flat = jnp.concatenate([block[8 * h : 8 * h + 8] for h in range(4)], axis=1).astype(BF16)
-        acc += jnp.dot(flat, w_buf[n * 512 : (n + 1) * 512, :], preferred_element_type=F32)
+        rows = pl.ds(pl.multiple_of(n * 512, 512), 512)
+        return jnp.dot(flat, w_buf[rows, :], preferred_element_type=F32)
+
+    loads[7].wait()
+    acc = project(p)
+    for n, k in reversed(tuple(enumerate(p_steps))):
+        source = p_index((4 - k[0], k[1]))
+        wait(abuf.at[source], recv_sem, 7 + n)
+        acc += project(source)
     xbuf[x] = acc
     for k in x_steps:
         send(xbuf.at[x], xbuf.at[x], 6, x_peer(k))
     wait(xbuf.at[pl.ds(0, XS - 1)], recv_sem, 6)
     out_ref[...] = ((xbuf[0] + xbuf[1]) + (xbuf[2] + xbuf[3])).astype(out_ref.dtype)
 
-    wait(zq.at[pl.ds(0, PLANES - 1)], send_sem, 0)
-    wait(qbuf.at[pl.ds(0, LOCAL - 1)], send_sem, 1)
+    wait(pbuf.at[pl.ds(0, LOCAL - 1)], send_sem, 0)
+    wait(zq.at[pl.ds(0, PLANES - 1)], send_sem, 1)
     wait(rbuf.at[pl.ds(0, LOCAL - 1)], send_sem, 2)
     wait(zs.at[pl.ds(0, PLANES - 1)], send_sem, 3)
     wait(zo.at[pl.ds(0, PLANES - 1)], send_sem, 4)
@@ -239,31 +242,36 @@
 
 def shards(queries, new_keys, new_values, keys, values, page_table, lengths, out_weight):
     vmem = pl.BlockSpec(memory_space=pltpu.VMEM)
-    smem = pl.BlockSpec(memory_space=pltpu.SMEM)
     hbm = pl.BlockSpec(memory_space=pl.ANY)
     return pl.pallas_call(
         kernel,
         out_shape=jax.ShapeDtypeStruct((ROWS, out_weight.shape[1]), BF16),
-        in_specs=[vmem, vmem, vmem, vmem, smem, hbm, hbm, hbm],
+        in_specs=[hbm] * 8,
         out_specs=vmem,
         scratch_shapes=[
+            pltpu.VMEM(queries.shape, BF16),
+            pltpu.VMEM(new_keys.shape, BF16),
+            pltpu.VMEM(new_values.shape, BF16),
+            pltpu.VMEM(page_table.shape, jnp.int32),
+            pltpu.SMEM(lengths.shape, jnp.int32),
             pltpu.VMEM(keys.shape, BF16),
             pltpu.VMEM(values.shape, BF16),
             pltpu.VMEM(out_weight.shape, BF16),
-            pltpu.VMEM((PLANES, 8, 128), F32),
-            pltpu.VMEM((LOCAL, 32, 128), F32),
+            pltpu.VMEM((LOCAL, 8, 128), F32),
+            pltpu.VMEM((PLANES, 16, 128), BF16),
             pltpu.VMEM((LOCAL, 32, 128), F32),
             pltpu.VMEM((LOCAL, 32, 128), F32),
             pltpu.VMEM((PLANES, 32, 128), BF16),
             pltpu.VMEM((PLANES, 1, 128), F32),
             pltpu.VMEM((LOCAL, 32, 128), BF16),
             pltpu.VMEM((XS, ROWS, 128), F32),
-            pltpu.SemaphoreType.DMA((3,)),
+            pltpu.SemaphoreType.DMA((8,)),
             pltpu.SemaphoreType.DMA((7,)),
-            pltpu.SemaphoreType.DMA((7,)),
+            pltpu.SemaphoreType.DMA((14,)),
+            pltpu.SemaphoreType.REGULAR,
         ],
         compiler_params=pltpu.CompilerParams(
-            collective_id=0, has_side_effects=True, vmem_limit_bytes=48 * 1024 * 1024
+            collective_id=0, has_side_effects=True, vmem_limit_bytes=64 * 1024 * 1024
         ),
     )(queries, new_keys, new_values, page_table, lengths, keys, values, out_weight)
 

time: 59.5 us -> 49.9 us (0.84)
  local copies, waits for them, and re-layouts: 7.65 us -> 1.26 us
  Pallas kernels: 51.5 us -> 48.5 us
    unnamed x17 -> x1, local copies, waits for them, and re-layouts: 7.65 us -> 1.26 us
    pallas_call x1, Pallas kernels: 51.5 us -> 48.5 us  [shards(): pl.pallas_call(kernel, out_shape=jax.ShapeDtypeStruct((ROWS, out_weight.s...]
where the time goes in v2:
time: 49.9 us; the launch traced here: 49.7 us
  Pallas kernels  48.5 us (97%)
  local copies, waits for them, and re-layouts  1.26 us (3%)
    pallas_call x1, Pallas kernels, shards(): pl.pallas_call(kernel, out_shape=jax.ShapeDtypeStruct((ROWS, out_weight.s...  48.5 us
    unnamed x1, local copies, waits for them, and re-layouts  1.26 us

profile of v2, /device:TPU:1, one launch (start us, length us, event | category | flops | bytes accessed | tf_op | source)
XLA Modules:
  0.0 49.7 jit_solution(12769526680153742925)
XLA Ops:
  0.0 48.5 %shard_map.82 = bf16[8,128]{1,0:T(8,128)(2,1)} custom-call(bf16[8,32]{1,0:T(8,128)(2,1)} %q_hbm.1, bf16[8,256]{1,0:T(8,128)(2,1)} %nk_hbm.1, bf16[8,256]{1,0:T(8,128)(2,1)} %nv_hbm.1, s32[8,64]{1,0:T(8,128)} %pt_hbm.1, s32[8]{0:T(128)} %len_hbm.1, bf16[4,512,256]{2,1,0:T(8,128)(2,1)} %k_hbm.1, bf16[4,512,256]{2,1,0:T(8,128)(2,1)} %v_hbm.1, ...), custom_call_target="tpu_custom_call" | custom-call | tf_op jit(solution)/shard_map/pallas_call | solution.py:246
  48.5 1.3 %copy.10 = bf16[8,128]{1,0:T(8,128)(2,1)} copy(bf16[8,128]{1,0:T(8,128)(2,1)} %shard_map.82) | data formatting | bytes 4096

commit v3 on v2

--- a/solution.py
+++ b/solution.py
@@ -26,7 +26,7 @@
 
 def kernel(
     q_hbm, nk_hbm, nv_hbm, pt_hbm, len_hbm, k_hbm, v_hbm, w_hbm, out_ref,
-    q_ref, nk_ref, nv_ref, pt_ref, len_ref, k_buf, v_buf, w_buf, pbuf, zq, sbuf, rbuf, zo, zs, abuf, xbuf,
+    q_ref, nk_ref, nv_ref, pt_ref, len_ref, k_buf, v_buf, w_buf, pbuf, zq, tbuf, ubuf, sbuf, rbuf, zo, zs, abuf, xbuf,
     load_sem, send_sem, recv_sem, ready_sem,
 ):
     i = lax.axis_index("seq")
@@ -94,7 +94,7 @@
         load.wait()
     lane64 = iota((128, 64), 1)
     rho = iota((128, 64), 0)
-    my_slot = i * SLOTS + ((rho >> 2) & 3)
+    my_slot = i * SLOTS + (rho >> 5)
     plane_slot = z * (LOCAL * SLOTS) + (rho >> 2)
     row_acc = jnp.zeros((128, 64), F32)
     live_acc = jnp.zeros((128, 64), F32)
@@ -111,12 +111,11 @@
 
     rho1 = iota((128, 1), 0)
     tau1 = iota((32, 1), 0)
-    head = jnp.concatenate([4 * (rho1 >> 4) + (rho1 & 3), 4 * p + (tau1 >> 3)], axis=0)
+    head = jnp.concatenate([rho1 & 31, 4 * p + (tau1 >> 3)], axis=0)
     row = jnp.concatenate([row_of, tau1 & 7], axis=0)
     start = (head >> 1) * 16 + (head & 1) * 8 + row
     select = (iota((160, 256), 1) == start).astype(F32).astype(BF16)
     l0, l1 = iota((128, 128), 0), iota((128, 128), 1)
-    slot_of = (rho1 >> 2) & 3
     match = ((l0 & 3) == ((l1 >> 3) & 3)) & (plane_row == (l1 & 7))
     first_kv = p < 4
     nk = jnp.where(first_kv, nk_ref[:, :HD].astype(F32), nk_ref[:, HD:].astype(F32))
@@ -137,68 +136,69 @@
     fresh_queries = queries[128:]
     queries = queries[:128]
 
+    scale = 1.0 / math.sqrt(HD)
+    low_head = iota((32, HD), 0) < 16
+    offset = iota((32, PAGE), 1)
+    stat_lane = iota((32, HD), 1) < 64
     loads[5].wait()
-    scores = jnp.zeros((128, PAGE), F32)
-    first_half = rho1 < 64
+    weights = []
     for s in range(SLOTS):
-        here = slot_of == s
+        mine = queries[32 * s : 32 * s + 32]
         block = jnp.concatenate(
-            [
-                jnp.where(here & first_half, queries, 0.0),
-                jnp.where(here & jnp.logical_not(first_half), queries, 0.0),
-            ],
-            axis=1,
+            [jnp.where(low_head, mine, 0.0), jnp.where(low_head, 0.0, mine)], axis=1
         ).astype(BF16)
-        scores += lax.dot_general(
+        scores = lax.dot_general(
             block, k_buf[s], (((1,), (1,)), ((), ())), preferred_element_type=F32
         )
-    scale = 1.0 / math.sqrt(HD)
-    live = iota((128, PAGE), 1) < live_of
-    masked = jnp.where(live, scores * scale, NEG)
-    page_max = jnp.max(masked, axis=1, keepdims=True)
-    weights = jnp.where(live, jnp.exp(masked - page_max), 0.0)
-    page_total = jnp.sum(weights, axis=1, keepdims=True)
+        live = offset < live_of[32 * s : 32 * s + 32]
+        masked = jnp.where(live, scores * scale, NEG)
+        page_max = jnp.max(masked, axis=1, keepdims=True)
+        weight = jnp.where(live, jnp.exp(masked - page_max), 0.0)
+        weights.append(weight.astype(BF16))
+        stats = jnp.where(stat_lane, page_max, jnp.sum(weight, axis=1, keepdims=True))
+        for n in range(LOCAL):
+            tbuf[n, 4 * s : 4 * s + 4, :] = stats[4 * n : 4 * n + 4]
+    for k in p_steps:
+        send(tbuf.at[p_index(k)], ubuf.at[p], 2, p_peer(k))
+    ubuf[p] = tbuf[p]
     loads[6].wait()
-    outs = jnp.zeros((128, 2 * HD), F32)
     for s in range(SLOTS):
-        outs += jnp.dot(
-            jnp.where(slot_of == s, weights, 0.0).astype(BF16), v_buf[s], preferred_element_type=F32
-        )
-    stats = jnp.where(l1 < 64, page_max, page_total)
-    for n in range(LOCAL):
-        half = n // 4
-        sbuf[n, 0:16, :] = outs[n * 16 : (n + 1) * 16, half * HD : (half + 1) * HD]
-        sbuf[n, 16:32, :] = stats[n * 16 : (n + 1) * 16]
+        outs = jnp.dot(weights[s], v_buf[s], preferred_element_type=F32)
+        for n in range(LOCAL):
+            half = n // 4
+            sbuf[n, 4 * s : 4 * s + 4, :] = outs[4 * n : 4 * n + 4, half * HD : (half + 1) * HD]
     for k in p_steps:
-        send(sbuf.at[p_index(k)], rbuf.at[p], 2, p_peer(k))
+        send(sbuf.at[p_index(k)], rbuf.at[p], 3, p_peer(k))
     rbuf[p] = sbuf[p]
     fresh_scores = jnp.sum(fresh_queries * nk, axis=1, keepdims=True) * scale
-    wait(rbuf.at[pl.ds(0, LOCAL - 1)], recv_sem, 2)
-
-    parts = rbuf[:, 0:16, :].reshape(128, 128)
-    stats = rbuf[:, 16:32, :].reshape(128, 128)
+
+    wait(ubuf.at[pl.ds(0, LOCAL - 1)], recv_sem, 2)
+    stats = ubuf[...].reshape(128, 128)
     turned = pltpu.roll(stats, 64, 1)
     part_max = jnp.where(l1 < 64, stats, turned)
     part_total = jnp.where(l1 < 64, turned, stats)
     plane_max = jnp.max(jnp.where(match, part_max, NEG), axis=0, keepdims=True)
     factor = jnp.where(match, jnp.exp(part_max - plane_max), 0.0)
     plane_total = jnp.sum(factor * part_total, axis=0, keepdims=True)
-    merged = jnp.dot(
-        factor.T[:32], parts, preferred_element_type=F32, precision=lax.Precision.HIGHEST
-    )
-    zo[z] = merged.astype(BF16)
     lane1 = iota((1, 128), 1)
     zs[z] = jnp.where(lane1 < 32, plane_max, plane_total)
     for k in z_steps:
-        send(zs.at[z], zs.at[z], 3, z_peer(k))
-        send(zo.at[z], zo.at[z], 4, z_peer(k))
-    wait(zs.at[pl.ds(0, PLANES - 1)], recv_sem, 3)
-    wait(zo.at[pl.ds(0, PLANES - 1)], recv_sem, 4)
-
-    table = jnp.full((128, 128), NEG, F32)
+        send(zs.at[z], zs.at[z], 4, z_peer(k))
+    factor = factor.T[:32]
+    wait(rbuf.at[pl.ds(0, LOCAL - 1)], recv_sem, 3)
+    merged = jnp.dot(
+        factor, rbuf[...].reshape(128, 128), preferred_element_type=F32, precision=lax.Precision.HIGHEST
+    )
+    zo[z] = merged.astype(BF16)
+    for k in z_steps:
+        send(zo.at[z], zo.at[z], 5, z_peer(k))
+
+    wait(zs.at[pl.ds(0, PLANES - 1)], recv_sem, 4)
+    row16 = iota((16, 128), 0)
+    table = jnp.zeros((PLANES, 128), F32)
     for n in range(PLANES):
-        table = jnp.where(l0 == n, zs[n], table)
-    table = table.T
+        table = jnp.where(row16 == n, zs[n], table)
+    table = jnp.concatenate([table, jnp.zeros((128 - PLANES, 128), F32)], axis=0).T
     lane32 = iota((32, 128), 1)
     maxima = jnp.where(lane32 < PLANES, table[:32], NEG)
     totals = jnp.where(lane32 < PLANES, table[32:64], 0.0)
@@ -206,12 +206,16 @@
     factor = jnp.exp(maxima - top)
     fresh_factor = jnp.exp(fresh_scores - top)
     total = jnp.sum(factor * totals, axis=1, keepdims=True) + fresh_factor
+    shares = [
+        jnp.broadcast_to(factor[:, n : n + 1], (32, 128)) for n in range(PLANES)
+    ]
     mixed = fresh_factor * nv
+    wait(zo.at[pl.ds(0, PLANES - 1)], recv_sem, 5)
     for n in range(PLANES):
-        mixed += factor[:, n : n + 1] * zo[n].astype(F32)
+        mixed += shares[n] * zo[n].astype(F32)
     abuf[p] = (mixed / total).astype(BF16)
     for n, k in enumerate(p_steps):
-        send(abuf.at[p], abuf.at[p], 5, p_peer(k), 7 + n)
+        send(abuf.at[p], abuf.at[p], 6, p_peer(k), 8 + n)
 
     def project(n):
         block = abuf[n].astype(F32)
@@ -223,29 +227,34 @@
     acc = project(p)
     for n, k in reversed(tuple(enumerate(p_steps))):
         source = p_index((4 - k[0], k[1]))
-        wait(abuf.at[source], recv_sem, 7 + n)
+        wait(abuf.at[source], recv_sem, 8 + n)
         acc += project(source)
     xbuf[x] = acc
     for k in x_steps:
-        send(xbuf.at[x], xbuf.at[x], 6, x_peer(k))
-    wait(xbuf.at[pl.ds(0, XS - 1)], recv_sem, 6)
+        send(xbuf.at[x], xbuf.at[x], 7, x_peer(k))
+    wait(xbuf.at[pl.ds(0, XS - 1)], recv_sem, 7)
     out_ref[...] = ((xbuf[0] + xbuf[1]) + (xbuf[2] + xbuf[3])).astype(out_ref.dtype)
 
     wait(pbuf.at[pl.ds(0, LOCAL - 1)], send_sem, 0)
     wait(zq.at[pl.ds(0, PLANES - 1)], send_sem, 1)
-    wait(rbuf.at[pl.ds(0, LOCAL - 1)], send_sem, 2)
-    wait(zs.at[pl.ds(0, PLANES - 1)], send_sem, 3)
-    wait(zo.at[pl.ds(0, PLANES - 1)], send_sem, 4)
-    wait(abuf.at[pl.ds(0, LOCAL - 1)], send_sem, 5)
-    wait(xbuf.at[pl.ds(0, XS - 1)], send_sem, 6)
+    wait(ubuf.at[pl.ds(0, LOCAL - 1)], send_sem, 2)
+    wait(rbuf.at[pl.ds(0, LOCAL - 1)], send_sem, 3)
+    wait(zs.at[pl.ds(0, PLANES - 1)], send_sem, 4)
+    wait(zo.at[pl.ds(0, PLANES - 1)], send_sem, 5)
+    wait(abuf.at[pl.ds(0, LOCAL - 1)], send_sem, 6)
+    wait(xbuf.at[pl.ds(0, XS - 1)], send_sem, 7)
 
 
 def shards(queries, new_keys, new_values, keys, values, page_table, lengths, out_weight):
+    operands = [
+        pltpu.with_memory_space_constraint(a, pltpu.HBM)
+        for a in (queries, new_keys, new_values, page_table, lengths, keys, values, out_weight)
+    ]
     vmem = pl.BlockSpec(memory_space=pltpu.VMEM)
     hbm = pl.BlockSpec(memory_space=pl.ANY)
     return pl.pallas_call(
         kernel,
-        out_shape=jax.ShapeDtypeStruct((ROWS, out_weight.shape[1]), BF16),
+        out_shape=pltpu.VMEM((ROWS, out_weight.shape[1]), BF16),
         in_specs=[hbm] * 8,
         out_specs=vmem,
         scratch_shapes=[
@@ -259,21 +268,23 @@
             pltpu.VMEM(out_weight.shape, BF16),
             pltpu.VMEM((LOCAL, 8, 128), F32),
             pltpu.VMEM((PLANES, 16, 128), BF16),
-            pltpu.VMEM((LOCAL, 32, 128), F32),
-            pltpu.VMEM((LOCAL, 32, 128), F32),
+            pltpu.VMEM((LOCAL, 16, 128), F32),
+            pltpu.VMEM((LOCAL, 16, 128), F32),
+            pltpu.VMEM((LOCAL, 16, 128), F32),
+            pltpu.VMEM((LOCAL, 16, 128), F32),
             pltpu.VMEM((PLANES, 32, 128), BF16),
             pltpu.VMEM((PLANES, 1, 128), F32),
             pltpu.VMEM((LOCAL, 32, 128), BF16),
             pltpu.VMEM((XS, ROWS, 128), F32),
             pltpu.SemaphoreType.DMA((8,)),
-            pltpu.SemaphoreType.DMA((7,)),
-            pltpu.SemaphoreType.DMA((14,)),
+            pltpu.SemaphoreType.DMA((8,)),
+            pltpu.SemaphoreType.DMA((15,)),
             pltpu.SemaphoreType.REGULAR,
         ],
         compiler_params=pltpu.CompilerParams(
-            collective_id=0, has_side_effects=True, vmem_limit_bytes=64 * 1024 * 1024
+            collective_id=0, has_side_effects=True, vmem_limit_bytes=40 * 1024 * 1024
         ),
-    )(queries, new_keys, new_values, page_table, lengths, keys, values, out_weight)
+    )(*operands)
 
 
 def solution(mesh):

time: 49.9 us -> 47.7 us (0.956)
  Pallas kernels: 48.5 us -> 47 us
  local copies, waits for them, and re-layouts: 1.26 us -> 0.58 us
    pallas_call x1, Pallas kernels: 48.5 us -> 47 us  [shards(): pl.pallas_call(kernel, out_shape=pltpu.VMEM((ROWS, out_weight.shape[1]),...]
    unnamed x1, local copies, waits for them, and re-layouts: 1.26 us -> 0.58 us
where the time goes in v3:
time: 47.7 us; the launch traced here: 47.6 us
  Pallas kernels  47 us (99%)
  local copies, waits for them, and re-layouts  0.58 us (1%)
    pallas_call x1, Pallas kernels, shards(): pl.pallas_call(kernel, out_shape=pltpu.VMEM((ROWS, out_weight.shape[1]),...  47 us

profile of v3, /device:TPU:1, one launch (start us, length us, event | category | flops | bytes accessed | tf_op | source)
XLA Modules:
  0.0 47.6 jit_solution(14129434404277216422)
XLA Ops:
  0.0 47.0 %shard_map.82 = bf16[8,128]{1,0:T(8,128)(2,1)S(1)} custom-call(bf16[8,32]{1,0:T(8,128)(2,1)} %q_hbm.1, bf16[8,256]{1,0:T(8,128)(2,1)} %nk_hbm.1, bf16[8,256]{1,0:T(8,128)(2,1)} %nv_hbm.1, s32[8,64]{1,0:T(8,128)} %pt_hbm.1, s32[8]{0:T(128)} %len_hbm.1, bf16[4,512,256]{2,1,0:T(8,128)(2,1)} %k_hbm.1, bf16[4,512,256]{2,1,0:T(8,128)(2,1)} %v_hbm.1, ...), custom_call_target="tpu_custom_call" | custom-call | tf_op jit(solution)/shard_map/pallas_call | solution.py:255
  47.0 0.6 %copy.10 = bf16[8,128]{1,0:T(8,128)(2,1)} copy(bf16[8,128]{1,0:T(8,128)(2,1)S(1)} %shard_map.82) | data formatting | bytes 4096

commit v4 on v3

--- a/solution.py
+++ b/solution.py
@@ -26,7 +26,7 @@
 
 def kernel(
     q_hbm, nk_hbm, nv_hbm, pt_hbm, len_hbm, k_hbm, v_hbm, w_hbm, out_ref,
-    q_ref, nk_ref, nv_ref, pt_ref, len_ref, k_buf, v_buf, w_buf, pbuf, zq, tbuf, ubuf, sbuf, rbuf, zo, zs, abuf, xbuf,
+    q_ref, nk_ref, nv_ref, pt_ref, len_ref, k_buf, v_buf, wp, pbuf, zq, tbuf, ubuf, sbuf, rbuf, zo, zs, hbuf, gbuf,
     load_sem, send_sem, recv_sem, ready_sem,
 ):
     i = lax.axis_index("seq")
@@ -36,7 +36,10 @@
 
     z_steps = sorted(range(1, PLANES), key=lambda k: -min(k, PLANES - k))
     p_steps = ((2, 0), (2, 1), (1, 0), (3, 0), (1, 1), (3, 1), (0, 1))
-    x_steps = (2, 1, 3)
+    g_steps = sorted(
+        ((a, b, c) for a in range(4) for b in range(2) for c in range(XS) if a or b or c),
+        key=lambda k: -min(k[0], 4 - k[0]) - min(k[2], XS - k[2]),
+    )
 
     def z_peer(k):
         return {"seq": lax.rem(z + k, PLANES) * LOCAL + p}
@@ -47,12 +50,11 @@
     def p_peer(k):
         return {"seq": z * LOCAL + p_index(k)}
 
-    def x_peer(k):
-        return {"mp": lax.rem(x + k, XS)}
+    def g_peer(k):
+        return {"seq": z * LOCAL + p_index(k), "mp": lax.rem(x + k[2], XS)}
 
     peers = [z_peer(k) for k in z_steps if min(k, PLANES - k) <= 4]
-    peers += [p_peer(k) for k in p_steps]
-    peers += [x_peer(k) for k in x_steps]
+    peers += [g_peer(k) for k in g_steps]
     barrier = pltpu.get_barrier_semaphore()
     for peer in peers:
         pl.semaphore_signal(barrier, inc=1, device_id=peer, device_id_type=MESH)
@@ -62,16 +64,16 @@
         for n, (src, dst) in enumerate(
             (
                 (q_hbm, q_ref), (pt_hbm, pt_ref), (len_hbm, len_ref), (nk_hbm, nk_ref),
-                (nv_hbm, nv_ref), (k_hbm, k_buf), (v_hbm, v_buf), (w_hbm, w_buf),
+                (nv_hbm, nv_ref), (k_hbm, k_buf), (v_hbm, v_buf),
             )
         )
     ]
     for load in loads:
         load.start()
 
-    def send(src, dst, n, peer, m=None):
+    def send(src, dst, n, peer):
         pltpu.make_async_remote_copy(
-            src_ref=src, dst_ref=dst, send_sem=send_sem.at[n], recv_sem=recv_sem.at[n if m is None else m],
+            src_ref=src, dst_ref=dst, send_sem=send_sem.at[n], recv_sem=recv_sem.at[n],
             device_id=peer, device_id_type=MESH,
         ).start()
 
@@ -130,6 +132,13 @@
     pl.semaphore_wait(ready_sem, 2)
     for k in z_steps:
         send(zq.at[z], zq.at[z], 1, z_peer(k))
+    def weight_rows(n):
+        return w_hbm.at[pl.ds(pl.multiple_of(n * 512, 512), 512), :]
+
+    own_rows = pltpu.make_async_copy(weight_rows(p), wp.at[p], load_sem.at[7])
+    own_rows.start()
+    for k in p_steps[2:]:
+        send(weight_rows(p_index(k)), wp.at[p], 6, p_peer(k))
     wait(zq.at[pl.ds(0, PLANES - 1)], recv_sem, 1)
 
     queries = jnp.dot(select, zq[...].reshape(256, 128), preferred_element_type=F32)
@@ -190,8 +199,12 @@
         factor, rbuf[...].reshape(128, 128), preferred_element_type=F32, precision=lax.Precision.HIGHEST
     )
     zo[z] = merged.astype(BF16)
-    for k in z_steps:
-        send(zo.at[z], zo.at[z], 5, z_peer(k))
+    for n in range(PLANES - 1):
+        plane = n + jnp.where(z <= n, 1, 0)
+        send(zo.at[z], zo.at[z], 5, {"seq": plane * LOCAL + p})
+
+    for k in p_steps[:2]:
+        send(weight_rows(p_index(k)), wp.at[p], 6, p_peer(k))
 
     wait(zs.at[pl.ds(0, PLANES - 1)], recv_sem, 4)
     row16 = iota((16, 128), 0)
@@ -213,27 +226,20 @@
     wait(zo.at[pl.ds(0, PLANES - 1)], recv_sem, 5)
     for n in range(PLANES):
         mixed += shares[n] * zo[n].astype(F32)
-    abuf[p] = (mixed / total).astype(BF16)
-    for n, k in enumerate(p_steps):
-        send(abuf.at[p], abuf.at[p], 6, p_peer(k), 8 + n)
-
-    def project(n):
-        block = abuf[n].astype(F32)
-        flat = jnp.concatenate([block[8 * h : 8 * h + 8] for h in range(4)], axis=1).astype(BF16)
-        rows = pl.ds(pl.multiple_of(n * 512, 512), 512)
-        return jnp.dot(flat, w_buf[rows, :], preferred_element_type=F32)
-
-    loads[7].wait()
-    acc = project(p)
-    for n, k in reversed(tuple(enumerate(p_steps))):
-        source = p_index((4 - k[0], k[1]))
-        wait(abuf.at[source], recv_sem, 8 + n)
-        acc += project(source)
-    xbuf[x] = acc
-    for k in x_steps:
-        send(xbuf.at[x], xbuf.at[x], 7, x_peer(k))
-    wait(xbuf.at[pl.ds(0, XS - 1)], recv_sem, 7)
-    out_ref[...] = ((xbuf[0] + xbuf[1]) + (xbuf[2] + xbuf[3])).astype(out_ref.dtype)
+    mixed = mixed / total
+    flat = jnp.concatenate([mixed[8 * h : 8 * h + 8] for h in range(4)], axis=1).astype(BF16)
+    own_rows.wait()
+    wait(wp.at[pl.ds(0, LOCAL - 1)], recv_sem, 6)
+    for n in range(LOCAL):
+        hbuf[n] = jnp.dot(flat, wp[n], preferred_element_type=F32)
+    for k in g_steps:
+        send(hbuf.at[p_index(k)], gbuf.at[x * LOCAL + p], 7, g_peer(k))
+    gbuf[x * LOCAL + p] = hbuf[p]
+    wait(gbuf.at[pl.ds(0, XS * LOCAL - 1)], recv_sem, 7)
+    terms = [gbuf[n] for n in range(XS * LOCAL)]
+    while len(terms) > 1:
+        terms = [a + b for a, b in zip(terms[::2], terms[1::2])]
+    out_ref[...] = terms[0].astype(out_ref.dtype)
 
     wait(pbuf.at[pl.ds(0, LOCAL - 1)], send_sem, 0)
     wait(zq.at[pl.ds(0, PLANES - 1)], send_sem, 1)
@@ -241,8 +247,8 @@
     wait(rbuf.at[pl.ds(0, LOCAL - 1)], send_sem, 3)
     wait(zs.at[pl.ds(0, PLANES - 1)], send_sem, 4)
     wait(zo.at[pl.ds(0, PLANES - 1)], send_sem, 5)
-    wait(abuf.at[pl.ds(0, LOCAL - 1)], send_sem, 6)
-    wait(xbuf.at[pl.ds(0, XS - 1)], send_sem, 7)
+    wait(wp.at[pl.ds(0, LOCAL - 1)], send_sem, 6)
+    wait(gbuf.at[pl.ds(0, XS * LOCAL - 1)], send_sem, 7)
 
 
 def shards(queries, new_keys, new_values, keys, values, page_table, lengths, out_weight):
@@ -265,7 +271,7 @@
             pltpu.SMEM(lengths.shape, jnp.int32),
             pltpu.VMEM(keys.shape, BF16),
             pltpu.VMEM(values.shape, BF16),
-            pltpu.VMEM(out_weight.shape, BF16),
+            pltpu.VMEM((LOCAL, out_weight.shape[0] // LOCAL, out_weight.shape[1]), BF16),
             pltpu.VMEM((LOCAL, 8, 128), F32),
             pltpu.VMEM((PLANES, 16, 128), BF16),
             pltpu.VMEM((LOCAL, 16, 128), F32),
@@ -274,11 +280,11 @@
             pltpu.VMEM((LOCAL, 16, 128), F32),
             pltpu.VMEM((PLANES, 32, 128), BF16),
             pltpu.VMEM((PLANES, 1, 128), F32),
-            pltpu.VMEM((LOCAL, 32, 128), BF16),
-            pltpu.VMEM((XS, ROWS, 128), F32),
+            pltpu.VMEM((LOCAL, ROWS, 128), F32),
+            pltpu.VMEM((XS * LOCAL, ROWS, 128), F32),
             pltpu.SemaphoreType.DMA((8,)),
             pltpu.SemaphoreType.DMA((8,)),
-            pltpu.SemaphoreType.DMA((15,)),
+            pltpu.SemaphoreType.DMA((8,)),
             pltpu.SemaphoreType.REGULAR,
         ],
         compiler_params=pltpu.CompilerParams(

time: 47.7 us -> 45.2 us (0.948)
  Pallas kernels: 47 us -> 44.4 us
    pallas_call x1, Pallas kernels: 47 us -> 44.4 us  [shards(): pl.pallas_call(kernel, out_shape=pltpu.VMEM((ROWS, out_weight.shape[1]),...]
where the time goes in v4:
time: 45.2 us; the launch traced here: 45 us
  Pallas kernels  44.4 us (98%)
  local copies, waits for them, and re-layouts  0.58 us (1%)
    pallas_call x1, Pallas kernels, shards(): pl.pallas_call(kernel, out_shape=pltpu.VMEM((ROWS, out_weight.shape[1]),...  44.4 us

profile of v4, /device:TPU:1, one launch (start us, length us, event | category | flops | bytes accessed | tf_op | source)
XLA Modules:
  0.0 45.0 jit_solution(17858763858573072862)
XLA Ops:
  0.0 44.4 %shard_map.82 = bf16[8,128]{1,0:T(8,128)(2,1)S(1)} custom-call(bf16[8,32]{1,0:T(8,128)(2,1)} %q_hbm.1, bf16[8,256]{1,0:T(8,128)(2,1)} %nk_hbm.1, bf16[8,256]{1,0:T(8,128)(2,1)} %nv_hbm.1, s32[8,64]{1,0:T(8,128)} %pt_hbm.1, s32[8]{0:T(128)} %len_hbm.1, bf16[4,512,256]{2,1,0:T(8,128)(2,1)} %k_hbm.1, bf16[4,512,256]{2,1,0:T(8,128)(2,1)} %v_hbm.1, ...), custom_call_target="tpu_custom_call" | custom-call | tf_op jit(solution)/shard_map/pallas_call | solution.py:261
  44.4 0.6 %copy.10 = bf16[8,128]{1,0:T(8,128)(2,1)} copy(bf16[8,128]{1,0:T(8,128)(2,1)S(1)} %shard_map.82) | data formatting | bytes 4096

commit v5 on v4

--- a/solution.py
+++ b/solution.py
@@ -139,6 +139,8 @@
     own_rows.start()
     for k in p_steps[2:]:
         send(weight_rows(p_index(k)), wp.at[p], 6, p_peer(k))
+    loads[5].wait()
+    loads[6].wait()
     wait(zq.at[pl.ds(0, PLANES - 1)], recv_sem, 1)
 
     queries = jnp.dot(select, zq[...].reshape(256, 128), preferred_element_type=F32)
@@ -149,7 +151,6 @@
     low_head = iota((32, HD), 0) < 16
     offset = iota((32, PAGE), 1)
     stat_lane = iota((32, HD), 1) < 64
-    loads[5].wait()
     weights = []
     for s in range(SLOTS):
         mine = queries[32 * s : 32 * s + 32]
@@ -170,7 +171,6 @@
     for k in p_steps:
         send(tbuf.at[p_index(k)], ubuf.at[p], 2, p_peer(k))
     ubuf[p] = tbuf[p]
-    loads[6].wait()
     for s in range(SLOTS):
         outs = jnp.dot(weights[s], v_buf[s], preferred_element_type=F32)
         for n in range(LOCAL):
@@ -191,12 +191,19 @@
     plane_total = jnp.sum(factor * part_total, axis=0, keepdims=True)
     lane1 = iota((1, 128), 1)
     zs[z] = jnp.where(lane1 < 32, plane_max, plane_total)
-    for k in z_steps:
-        send(zs.at[z], zs.at[z], 4, z_peer(k))
+    for n in range(PLANES - 1):
+        plane = n + jnp.where(z <= n, 1, 0)
+        send(zs.at[z], zs.at[z], 4, {"seq": plane * LOCAL + p})
     factor = factor.T[:32]
+    high = factor.astype(BF16)
+    low = (factor - high.astype(F32)).astype(BF16)
+    factor = jnp.concatenate([high, high, low], axis=1)
     wait(rbuf.at[pl.ds(0, LOCAL - 1)], recv_sem, 3)
+    parts = rbuf[...].reshape(128, 128)
+    high = parts.astype(BF16)
+    low = (parts - high.astype(F32)).astype(BF16)
     merged = jnp.dot(
-        factor, rbuf[...].reshape(128, 128), preferred_element_type=F32, precision=lax.Precision.HIGHEST
+        factor, jnp.concatenate([high, low, high], axis=0), preferred_element_type=F32
     )
     zo[z] = merged.astype(BF16)
     for n in range(PLANES - 1):
@@ -230,10 +237,18 @@
     flat = jnp.concatenate([mixed[8 * h : 8 * h + 8] for h in range(4)], axis=1).astype(BF16)
     own_rows.wait()
     wait(wp.at[pl.ds(0, LOCAL - 1)], recv_sem, 6)
-    for n in range(LOCAL):
-        hbuf[n] = jnp.dot(flat, wp[n], preferred_element_type=F32)
-    for k in g_steps:
-        send(hbuf.at[p_index(k)], gbuf.at[x * LOCAL + p], 7, g_peer(k))
+    me = (p >> 1) * 8 + x * 2 + 1 - (p & 1)
+    for n in range(0, LOCAL, 2):
+        pair = jnp.dot(
+            flat, jnp.concatenate([wp[n], wp[n + 1]], axis=1), preferred_element_type=F32
+        )
+        hbuf[n] = pair[:, :128]
+        hbuf[n + 1] = pair[:, 128:]
+        for m in range(max(0, 4 * n - 1), 4 * n + 7):
+            other = m + jnp.where(me <= m, 1, 0)
+            column = (other >> 3) * 2 + 1 - (other & 1)
+            peer = {"seq": z * LOCAL + column, "mp": (other >> 1) & 3}
+            send(hbuf.at[column], gbuf.at[x * LOCAL + p], 7, peer)
     gbuf[x * LOCAL + p] = hbuf[p]
     wait(gbuf.at[pl.ds(0, XS * LOCAL - 1)], recv_sem, 7)
     terms = [gbuf[n] for n in range(XS * LOCAL)]

time: 45.2 us -> 44.7 us (0.989)
  no operation moved by 1% of the time
where the time goes in v5:
time: 44.7 us; the launch traced here: 44.6 us
  Pallas kernels  44 us (98%)
  local copies, waits for them, and re-layouts  0.58 us (1%)
    pallas_call x1, Pallas kernels, shards(): pl.pallas_call(kernel, out_shape=pltpu.VMEM((ROWS, out_weight.shape[1]),...  44 us

profile of v5, /device:TPU:1, one launch (start us, length us, event | category | flops | bytes accessed | tf_op | source)
XLA Modules:
  0.0 44.6 jit_solution(3457900607431496752)
XLA Ops:
  0.0 44.0 %shard_map.82 = bf16[8,128]{1,0:T(8,128)(2,1)S(1)} custom-call(bf16[8,32]{1,0:T(8,128)(2,1)} %q_hbm.1, bf16[8,256]{1,0:T(8,128)(2,1)} %nk_hbm.1, bf16[8,256]{1,0:T(8,128)(2,1)} %nv_hbm.1, s32[8,64]{1,0:T(8,128)} %pt_hbm.1, s32[8]{0:T(128)} %len_hbm.1, bf16[4,512,256]{2,1,0:T(8,128)(2,1)} %k_hbm.1, bf16[4,512,256]{2,1,0:T(8,128)(2,1)} %v_hbm.1, ...), custom_call_target="tpu_custom_call" | custom-call | tf_op jit(solution)/shard_map/pallas_call | solution.py:276
  44.0 0.6 %copy.10 = bf16[8,128]{1,0:T(8,128)(2,1)} copy(bf16[8,128]{1,0:T(8,128)(2,1)S(1)} %shard_map.82) | data formatting | bytes 4096

commit v6 on v5

--- a/solution.py
+++ b/solution.py
@@ -226,14 +226,14 @@
     factor = jnp.exp(maxima - top)
     fresh_factor = jnp.exp(fresh_scores - top)
     total = jnp.sum(factor * totals, axis=1, keepdims=True) + fresh_factor
+    factor = factor / total
     shares = [
         jnp.broadcast_to(factor[:, n : n + 1], (32, 128)) for n in range(PLANES)
     ]
-    mixed = fresh_factor * nv
+    mixed = (fresh_factor / total) * nv
     wait(zo.at[pl.ds(0, PLANES - 1)], recv_sem, 5)
     for n in range(PLANES):
         mixed += shares[n] * zo[n].astype(F32)
-    mixed = mixed / total
     flat = jnp.concatenate([mixed[8 * h : 8 * h + 8] for h in range(4)], axis=1).astype(BF16)
     own_rows.wait()
     wait(wp.at[pl.ds(0, LOCAL - 1)], recv_sem, 6)

time: 44.7 us -> 44.7 us (level)
  no operation moved by 1% of the time
where the time goes in v6:
time: 44.7 us; the launch traced here: 44.6 us
  Pallas kernels  44 us (98%)
  local copies, waits for them, and re-layouts  0.58 us (1%)
    pallas_call x1, Pallas kernels, shards(): pl.pallas_call(kernel, out_shape=pltpu.VMEM((ROWS, out_weight.shape[1]),...  44 us

profile of v6, /device:TPU:1, one launch (start us, length us, event | category | flops | bytes accessed | tf_op | source)
XLA Modules:
  0.0 44.6 jit_solution(8939986126348939534)
XLA Ops:
  0.0 44.0 %shard_map.82 = bf16[8,128]{1,0:T(8,128)(2,1)S(1)} custom-call(bf16[8,32]{1,0:T(8,128)(2,1)} %q_hbm.1, bf16[8,256]{1,0:T(8,128)(2,1)} %nk_hbm.1, bf16[8,256]{1,0:T(8,128)(2,1)} %nv_hbm.1, s32[8,64]{1,0:T(8,128)} %pt_hbm.1, s32[8]{0:T(128)} %len_hbm.1, bf16[4,512,256]{2,1,0:T(8,128)(2,1)} %k_hbm.1, bf16[4,512,256]{2,1,0:T(8,128)(2,1)} %v_hbm.1, ...), custom_call_target="tpu_custom_call" | custom-call | tf_op jit(solution)/shard_map/pallas_call | solution.py:276
  44.0 0.6 %copy.10 = bf16[8,128]{1,0:T(8,128)(2,1)} copy(bf16[8,128]{1,0:T(8,128)(2,1)S(1)} %shard_map.82) | data formatting | bytes 4096
